TPU v7x, 32 devices: a whole 2x2x4 slice. The times are simulated.
32 devices in a mesh: task: 4 (over y, core), row: 8 (over z, x).
Axes of the slice: x: 2, y: 2, z: 4, core: 2. Of those that a mesh axis runs over, the one named last changes fastest.
Arguments:
- deltas: bfloat16 [8, 25600, 5120], P('task', 'row'), may hold values from -20 to 20, as said below
- sketch: bfloat16 [25600, 128], P('row'), may hold values from -0.0390625 to 0.0390625
Outputs:
- merged: bfloat16 [25600, 5120], P('row', 'task')
Inputs may be any that keep to these rules, and one draw needn't show every extreme that they name: Real-valued deltas; the tasks share part of their structure.
All inputs are finite; a program needn't handle non-finite values.
Results may differ from a plain program's by a relative error of at most 0.04.
Values may be sent and summed in bfloat16 or wider, within the bound.
A program may use at most 192 MiB of HBM per device.

v0:
```python
import jax
import jax.numpy as jnp
from jax import lax
from jax.sharding import PartitionSpec as P

NS_STEPS = 5


def body(deltas, sketch):
    local_tasks = deltas.shape[0]
    local_rows = deltas.shape[1]
    model_width = deltas.shape[2]
    rank_width = sketch.shape[1]
    group_count = lax.axis_size("task")
    row_devices = lax.axis_size("row")
    basis_rows_dev = model_width // row_devices
    group_width = local_tasks * rank_width
    basis_width = group_width * group_count
    gram_rows_dev = basis_width // row_devices
    terms = jnp.einsum("tmk,mr->ktr", deltas, sketch, preferred_element_type=jnp.float32)
    basis_local = lax.psum_scatter(
        terms.reshape(basis_rows_dev * lax.axis_size("row"), group_width).astype(jnp.bfloat16),
        "row",
        scatter_dimension=0,
        tiled=True,
    )
    basis_block = lax.all_gather(basis_local, "task", axis=1, tiled=True)
    gram_local = lax.psum_scatter(
        jnp.einsum(
            "kc,kp->cp", basis_block, basis_local, preferred_element_type=jnp.float32
        ).astype(jnp.bfloat16),
        "row",
        scatter_dimension=0,
        tiled=True,
    ).astype(jnp.float32)
    gram_own = lax.all_gather(gram_local.astype(jnp.bfloat16), "task", axis=1, tiled=True).astype(
        gram_local.dtype
    )
    frob = jnp.sqrt(lax.psum(jnp.sum(gram_own * gram_own), "row"))
    rows_y = (gram_own / frob).astype(jnp.bfloat16)
    first_row = lax.axis_index("row") * gram_rows_dev
    row_ids = lax.broadcasted_iota(jnp.int32, (gram_rows_dev, basis_width), 0) + first_row
    col_ids = lax.broadcasted_iota(jnp.int32, (gram_rows_dev, basis_width), 1)
    identity_rows = jnp.where(row_ids == col_ids, 1.0, 0.0).astype(jnp.float32)
    turn_rows = ((3.0 * identity_rows - rows_y.astype(jnp.float32)) * 0.5).astype(jnp.bfloat16)
    whole_turn = lax.all_gather(turn_rows, "row", axis=0, tiled=True)
    rows_y = jnp.dot(rows_y, whole_turn, preferred_element_type=jnp.float32).astype(jnp.bfloat16)
    rows_z = turn_rows
    for iteration in range(1, NS_STEPS):
        whole_y, whole_z = (
            lax.all_gather(rows_y, "row", axis=0, tiled=True),
            lax.all_gather(rows_z, "row", axis=0, tiled=True),
        )
        turn = (
            (3.0 * identity_rows - jnp.dot(rows_z, whole_y, preferred_element_type=jnp.float32))
            * 0.5
        ).astype(jnp.bfloat16)
        if iteration + 1 < NS_STEPS:
            rows_y = jnp.dot(turn, whole_y, preferred_element_type=jnp.float32).astype(jnp.bfloat16)
        rows_z = jnp.dot(turn, whole_z, preferred_element_type=jnp.float32).astype(jnp.bfloat16)
    inverse_root = lax.all_gather(rows_z, "row", axis=0, tiled=True)
    basis_whole = lax.all_gather(basis_block, "row", axis=0, tiled=True)
    task_total = local_tasks * group_count
    coeff_part = jnp.zeros((local_rows, basis_width), jnp.float32)
    for task_slot in range(local_tasks):
        coeff_part = coeff_part + jnp.dot(
            deltas[task_slot], basis_whole, preferred_element_type=jnp.float32
        )
    coeff = (
        lax.psum(coeff_part.astype(jnp.bfloat16), "task").astype(jnp.float32) / task_total
    ).astype(jnp.bfloat16)
    second = jnp.dot(coeff, inverse_root, preferred_element_type=jnp.float32).astype(jnp.bfloat16)
    third = (jnp.dot(second, inverse_root, preferred_element_type=jnp.float32) / frob).astype(
        jnp.bfloat16
    )
    column_width = model_width // group_count
    column_basis = lax.dynamic_slice_in_dim(
        basis_whole, lax.axis_index("task") * column_width, column_width, 0
    )
    return jnp.einsum("mc,kc->mk", third, column_basis, preferred_element_type=jnp.float32).astype(
        jnp.bfloat16
    )


def solution(mesh):
    return jax.shard_map(
        body,
        mesh=mesh,
        in_specs=(P("task", "row", None), P("row", None)),
        out_specs=P("row", "task"),
        check_vma=False,
    )
```

profile of v0, /device:TPU:0, one launch (start us, length us, event | category | flops | bytes accessed | tf_op | source)
XLA Modules:
  0.0 988.9 jit_solution(3099222203837600109)
XLA Ops:
  7.7 24.2 %convolution_convert_fusion.2 = bf16[128,2,5120]{2,0,1:T(8,128)(2,1)S(1)} fusion(bf16[2,3200,5120]{2,1,0:T(8,128)(2,1)} %param.2, bf16[3200,128]{1,0:T(8,128)(2,1)S(1)} %copy-done), kind=kOutput, calls=%fused_computation.15 | convolution fusion | flops 8389918720 | bytes 68976640 | tf_op jit(solution)/shard_map/tmk,mr->ktr/dot_general | solution.py:20
  31.9 2.6 copy.7
  34.6 73.2 %reduce-scatter.7.cloned.1.call-done = bf16[640,256]{1,0:T(8,128)(2,1)} async-done(((bf16[5120,256]{1,0:T(8,128)(2,1)}), bf16[640,256]{1,0:T(8,128)(2,1)}) %reduce-scatter.7.cloned.1.call-update) | async-done | bytes 327696
  107.8 1.9 copy.8
  109.7 17.2 %all-gather.12.cloned.1.call-done = bf16[640,1024]{0,1:T(8,128)(2,1)} async-done(((bf16[640,256]{0,1:T(8,128)(2,1)}), bf16[640,1024]{0,1:T(8,128)(2,1)}) %all-gather.12.cloned.1.call-update) | async-done | bytes 1310736 | tf_op jit(solution)/shard_map/all_gather | solution.py:27
  127.0 2.7 convolution_convert_fusion.3
  129.8 62.9 %reduce-scatter.5.cloned.1.call-done = bf16[128,256]{1,0:T(8,128)(2,1)} async-done(((bf16[1024,256]{1,0:T(8,128)(2,1)}), bf16[128,256]{1,0:T(8,128)(2,1)}) %reduce-scatter.5.cloned.1.call-update) | async-done | bytes 65552 | tf_op jit(solution)/shard_map/reduce_scatter | solution.py:28
  192.7 6.0 all_gather.39
  199.4 20.1 %psum.15 = f32[]{:T(128)} all-reduce(f32[]{:T(128)} %fusion.25), channel_id=1, replica_groups=mesh['task'=4,'row'=8] {'row'}, use_global_device_ids=true, to_apply=%region_4.5 | all-reduce | flops 1 | bytes 8 | tf_op jit(solution)/shard_map/psum | solution.py:39
  221.1 46.6 %all-gather.16.cloned.1.call-done = bf16[1024,1024]{1,0:T(8,128)(2,1)} async-done(((bf16[128,1024]{1,0:T(8,128)(2,1)}), bf16[1024,1024]{1,0:T(8,128)(2,1)}) %all-gather.16.cloned.1.call-update) | async-done | bytes 2097168 | tf_op jit(solution)/shard_map/all_gather | solution.py:46
  267.7 2.7 convolution_convert_fusion.11
  270.6 47.9 %all-gather.18.cloned.1.call-done = bf16[1024,1024]{1,0:T(8,128)(2,1)} async-done(((bf16[128,1024]{1,0:T(8,128)(2,1)}), bf16[1024,1024]{1,0:T(8,128)(2,1)}) %all-gather.18.cloned.1.call-update) | async-done | bytes 2097168 | tf_op jit(solution)/shard_map/all_gather | solution.py:51
  318.5 2.1 fusion.20
  320.5 2.7 convolution_convert_fusion.9
  324.6 46.7 %all-gather.20.cloned.1.call-done = bf16[1024,1024]{1,0:T(8,128)(2,1)} async-done(((bf16[128,1024]{1,0:T(8,128)(2,1)}), bf16[1024,1024]{1,0:T(8,128)(2,1)}) %all-gather.20.cloned.1.call-update) | async-done | bytes 2097168 | tf_op jit(solution)/shard_map/all_gather | solution.py:51
  371.3 2.3 fusion.21
  373.6 1.2 convolution_convert_fusion.7
  374.8 46.6 %all-gather.22.cloned.1.call-done = bf16[1024,1024]{1,0:T(8,128)(2,1)} async-done(((bf16[128,1024]{1,0:T(8,128)(2,1)}), bf16[1024,1024]{1,0:T(8,128)(2,1)}) %all-gather.22.cloned.1.call-update) | async-done | bytes 2097168 | tf_op jit(solution)/shard_map/all_gather | solution.py:52
  421.4 2.7 convolution_convert_fusion.8
  424.8 46.7 %all-gather.24.cloned.1.call-done = bf16[1024,1024]{1,0:T(8,128)(2,1)} async-done(((bf16[128,1024]{1,0:T(8,128)(2,1)}), bf16[1024,1024]{1,0:T(8,128)(2,1)}) %all-gather.24.cloned.1.call-update) | async-done | bytes 2097168 | tf_op jit(solution)/shard_map/all_gather | solution.py:51
  471.6 2.3 fusion.22
  475.1 46.6 %all-gather.26.cloned.1.call-done = bf16[1024,1024]{1,0:T(8,128)(2,1)} async-done(((bf16[128,1024]{1,0:T(8,128)(2,1)}), bf16[1024,1024]{1,0:T(8,128)(2,1)}) %all-gather.26.cloned.1.call-update) | async-done | bytes 2097168 | tf_op jit(solution)/shard_map/all_gather | solution.py:52
  521.7 2.7 convolution_convert_fusion.6
  524.7 148.4 %all-gather.14.cloned.1.call-done = bf16[5120,1024]{0,1:T(8,128)(2,1)} async-done(((bf16[640,1024]{0,1:T(8,128)(2,1)}), bf16[5120,1024]{0,1:T(8,128)(2,1)}) %all-gather.14.cloned.1.call-update) | async-done | bytes 10485776 | tf_op jit(solution)/shard_map/all_gather | solution.py:62
  673.1 44.6 %fusion = f32[1024,3200]{1,0:T(8,128)} fusion(bf16[5120,1024]{0,1:T(8,128)(2,1)} %all-gather.14.cloned.1.call-done, bf16[2,3200,5120]{2,1,0:T(8,128)(2,1)} %param.2), kind=kOutput, calls=%fused_computation | convolution fusion | flops 33554432000 | bytes 56360960 | tf_op jit(solution)/shard_map/dot_general | solution.py:66
  717.8 43.2 %fusion.12 = bf16[3200,1024]{0,1:T(8,128)(2,1)} fusion(f32[1024,3200]{1,0:T(8,128)} %fusion, bf16[5120,1024]{0,1:T(8,128)(2,1)S(1)} %copy-done.7, bf16[2,3200,5120]{2,1,0:T(8,128)(2,1)} %param.2), kind=kOutput, calls=%fused_computation.14 | convolution fusion | flops 33560985600 | bytes 62914560 | tf_op jit(solution)/shard_map/dot_general | solution.py:66
  761.3 11.8 %all-gather.30.cloned.1.call-done = bf16[1024,1024]{1,0:T(8,128)(2,1)} async-done(((bf16[128,1024]{1,0:T(8,128)(2,1)}), bf16[1024,1024]{1,0:T(8,128)(2,1)}) %all-gather.30.cloned.1.call-update) | async-done | bytes 2097168 | tf_op jit(solution)/shard_map/all_gather | solution.py:52
  773.1 3.8 convolution_convert_fusion.4
  776.9 121.1 %all-reduce.2.cloned.1.call-done = bf16[3200,1024]{0,1:T(8,128)(2,1)} async-done(((bf16[3200,1024]{0,1:T(8,128)(2,1)}), bf16[3200,1024]{0,1:T(8,128)(2,1)}) %all-reduce.2.cloned.1.call-update) | async-done | bytes 6553616 | tf_op jit(solution)/shard_map/psum | solution.py:70
  898.0 51.7 %all-gather.32.cloned.1.call-done = bf16[1024,1024]{1,0:T(8,128)(2,1)} async-done(((bf16[128,1024]{1,0:T(8,128)(2,1)}), bf16[1024,1024]{1,0:T(8,128)(2,1)}) %all-gather.32.cloned.1.call-update) | async-done | bytes 2097168 | tf_op jit(solution)/shard_map/all_gather | solution.py:61
  949.7 12.3 %convolution_convert_fusion.1 = bf16[3200,1024]{1,0:T(8,128)(2,1)} fusion(bf16[1024,1024]{1,0:T(8,128)(2,1)} %all-gather.32.cloned.1.call-done, bf16[3200,1024]{0,1:T(8,128)(2,1)} %all-reduce.2.cloned.1.call-done), kind=kOutput, calls=%fused_computation.10 | convolution fusion | flops 6723993600 | bytes 15204352 | tf_op jit(solution)/shard_map/dot_general | solution.py:72
  962.0 20.3 %convolution_convert_fusion = bf16[3200,1280]{1,0:T(8,128)(2,1)} fusion(bf16[3200,1024]{1,0:T(8,128)(2,1)} %convolution_convert_fusion.1, bf16[1024,1024]{1,0:T(8,128)(2,1)S(1)} %copy-done.8, f32[]{:T(128)S(6)} %sqrt.3, bf16[5120,1024]{0,1:T(8,128)(2,1)} %all-gather.14.cloned.1.call-done, s32[]{:T(128)S(6)} %select_n.8), kind=kOutput, calls=%fused_computation.6 | convolution fusion | flops 15110144000 | bytes 19464200 | tf_op jit(solution)/shard_map/mc,kc->mk/dot_general | solution.py:80
  (52 shorter events, 6.8 us)
Async XLA Ops:
  6.5 1.1 copy-start
  6.5 101.2 %reduce-scatter.7.cloned.1.call-start = ((), (), s32[]{:S(2)}) async-start(), calls=%async_computation.15 | async-start | bytes 2949120
  34.5 92.5 %all-gather.12.cloned.1.call-start = ((), (), s32[]{:S(2)}) async-start(), calls=%async_computation.2 | async-start | bytes 1638400 | tf_op jit(solution)/shard_map/all_gather | solution.py:27
  109.7 83.0 %reduce-scatter.5.cloned.1.call-start = ((), (), s32[]{:S(2)}) async-start(), calls=%async_computation.5 | async-start | bytes 589824 | tf_op jit(solution)/shard_map/reduce_scatter | solution.py:28
  129.7 138.0 %all-gather.16.cloned.1.call-start = ((), (), s32[]{:S(2)}) async-start(), calls=%async_computation.6 | async-start | bytes 2359296 | tf_op jit(solution)/shard_map/all_gather | solution.py:46
  221.0 97.4 %copy-start.6 = (bf16[128,1024]{1,0:T(8,128)(2,1)S(1)}, bf16[128,1024]{1,0:T(8,128)(2,1)}, u32[]{:S(2)}) copy-start(bf16[128,1024]{1,0:T(8,128)(2,1)} %multiply_convert_fusion.2) | copy-start | bytes 786436
  221.1 97.4 %all-gather.18.cloned.1.call-start = ((), (), s32[]{:S(2)}) async-start(), calls=%async_computation.7 | async-start | bytes 2359296 | tf_op jit(solution)/shard_map/all_gather | solution.py:51
  270.5 52.9 %copy-start.2 = (bf16[1024,1024]{1,0:T(8,128)(2,1)S(1)}, bf16[1024,1024]{1,0:T(8,128)(2,1)}, u32[]{:S(2)}) copy-start(bf16[1024,1024]{1,0:T(8,128)(2,1)} %all-gather.16.cloned.1.call-done) | copy-start | bytes 6291460
  270.5 100.7 %all-gather.20.cloned.1.call-start = ((), (), s32[]{:S(2)}) async-start(), calls=%async_computation.8 | async-start | bytes 2359296 | tf_op jit(solution)/shard_map/all_gather | solution.py:51
  323.3 98.1 %all-gather.22.cloned.1.call-start = ((), (), s32[]{:S(2)}) async-start(), calls=%async_computation.9 | async-start | bytes 2359296 | tf_op jit(solution)/shard_map/all_gather | solution.py:52
  324.6 147.0 %all-gather.24.cloned.1.call-start = ((), (), s32[]{:S(2)}) async-start(), calls=%async_computation.10 | async-start | bytes 2359296 | tf_op jit(solution)/shard_map/all_gather | solution.py:51
  371.3 2.3 copy-start.4
  374.8 146.9 %all-gather.26.cloned.1.call-start = ((), (), s32[]{:S(2)}) async-start(), calls=%async_computation.11 | async-start | bytes 2359296 | tf_op jit(solution)/shard_map/all_gather | solution.py:52
  424.2 248.9 %all-gather.14.cloned.1.call-start = ((), (), s32[]{:S(2)}) async-start(), calls=%async_computation.3 | async-start | bytes 11796480 | tf_op jit(solution)/shard_map/all_gather | solution.py:62
  424.8 336.5 %all-gather.28.cloned.1.call-start = ((), (), s32[]{:S(2)}) async-start(), calls=%async_computation.12 | async-start | bytes 2359296 | tf_op jit(solution)/shard_map/all_gather | solution.py:51
  471.6 2.3 copy-start.3
  475.1 298.1 %all-gather.30.cloned.1.call-start = ((), (), s32[]{:S(2)}) async-start(), calls=%async_computation.13 | async-start | bytes 2359296 | tf_op jit(solution)/shard_map/all_gather | solution.py:52
  524.5 373.5 %all-reduce.2.cloned.1.call-start = ((), (), s32[]{:S(2)}) async-start(), calls=%async_computation.4 | async-start | bytes 13107200 | tf_op jit(solution)/shard_map/psum | solution.py:70
  673.1 44.7 %copy-start.7 = (bf16[5120,1024]{0,1:T(8,128)(2,1)S(1)}, bf16[5120,1024]{0,1:T(8,128)(2,1)}, u32[]{:S(2)}) copy-start(bf16[5120,1024]{0,1:T(8,128)(2,1)} %all-gather.14.cloned.1.call-done) | copy-start | bytes 31457284
  761.0 12.1 %copy-start.5 = (bf16[128,1024]{1,0:T(8,128)(2,1)S(1)}, bf16[128,1024]{1,0:T(8,128)(2,1)}, u32[]{:S(2)}) copy-start(bf16[128,1024]{1,0:T(8,128)(2,1)} %convolution_convert_fusion.6) | copy-start | bytes 786436
  761.0 188.7 %all-gather.32.cloned.1.call-start = ((), (), s32[]{:S(2)}) async-start(), calls=%async_computation.14 | async-start | bytes 2359296 | tf_op jit(solution)/shard_map/all_gather | solution.py:61
  949.7 12.3 %copy-start.8 = (bf16[1024,1024]{1,0:T(8,128)(2,1)S(1)}, bf16[1024,1024]{1,0:T(8,128)(2,1)}, u32[]{:S(2)}) copy-start(bf16[1024,1024]{1,0:T(8,128)(2,1)} %all-gather.32.cloned.1.call-done) | copy-start | bytes 6291460
  962.0 20.3 %copy-start.1 = (bf16[3200,128]{1,0:T(8,128)(2,1)S(1)}, bf16[3200,128]{1,0:T(8,128)(2,1)}, u32[]{:S(2)}) copy-start(bf16[3200,128]{1,0:T(8,128)(2,1)} %param.3) | copy-start | bytes 2457604
Sparse Core Ops, SparseCore 0:
  34.6 73.1 reduce-scatter.6
  109.8 17.1 all-gather.11
  130.3 62.3 reduce-scatter.4
  221.2 46.5 all-gather.15
  270.6 47.7 all-gather.17
  323.4 47.7 all-gather.19
  373.6 47.7 all-gather.21
  423.8 47.7 all-gather.23
  473.9 47.7 all-gather.25
  524.0 149.0 all-gather.13
  675.5 47.6 all-gather.27
  725.3 47.7 all-gather.29
  775.6 122.3 all-reduce.1
  900.2 49.4 all-gather.31
where the time goes:
time: 989 us
  waiting for transfers between devices  768 us (78%)
  matrix products  172 us (17%)
  blocking collectives  26 us (3%)
  between operations  14.1 us (1%)
    all_gather x1, waiting for transfers between devices, body(): basis_whole = lax.all_gather(basis_block, 'row', axis=0, tiled=True)  148 us
    all_gather x4, waiting for transfers between devices, body(): lax.all_gather(rows_y, 'row', axis=0, tiled=True)  141 us
    psum x1, waiting for transfers between devices, body(): lax.psum(coeff_part.astype(jnp.bfloat16), 'task').astype(jnp.float32)  121 us
    all_gather x3, waiting for transfers between devices, body(): lax.all_gather(rows_z, 'row', axis=0, tiled=True)  105 us
    dot_general x2, matrix products, body(): jnp.dot(deltas[task_slot], basis_whole, preferred_element_type=jnp.float32)  87.9 us
    unnamed x15, waiting for transfers between devices  74 us
    reduce_scatter x1, waiting for transfers between devices, body(): lax.psum_scatter(jnp.einsum('kc,kp->cp', basis_block, basis_local, prefer...  62.9 us
    all_gather x1, waiting for transfers between devices, body(): inverse_root = lax.all_gather(rows_z, 'row', axis=0, tiled=True)  51.7 us
  transfers between devices with their start and end apart: 14, of which 13 were waited for; matrix products, arithmetic and copies ran while one was open for 11% of the time, Pallas kernels for 0%

commit v1 on v0

v1 whole, which is shorter than its diff:
```python
import jax
import jax.numpy as jnp
from jax import lax
from jax.sharding import PartitionSpec as P

NS_STEPS = 5
ROW_CHUNKS = 4


def dot32(a, b):
    return jnp.dot(a, b, preferred_element_type=jnp.float32)


def dot16(a, b):
    return dot32(a, b).astype(jnp.bfloat16)


def swap(value, bit, size):
    return lax.ppermute(value, "task", [(i, i ^ bit) for i in range(size)])


def ring_order(size):
    return list(range(0, size, 2)) + list(range(size - 1 - size % 2, 0, -2))


def reduce_blocks(terms, order, place):
    size, rows = terms.shape[0], terms.shape[1]
    half = rows // 2
    table = jnp.array(order, jnp.int32)
    ahead = [(order[i], order[(i + 1) % size]) for i in range(size)]
    back = [(b, a) for a, b in ahead]

    def block(position, low):
        own = lax.dynamic_index_in_dim(terms, table[position % size], 0, keepdims=False)
        return own[:half] if low else own[half:]

    one = block(place - 1 + size, True)
    two = block(place + 1, False)
    for step in range(size - 1):
        one = lax.ppermute(one, "row", ahead)
        two = lax.ppermute(two, "row", back)
        one = one.astype(jnp.float32) + block(place - 2 - step + 2 * size, True).astype(jnp.float32)
        two = two.astype(jnp.float32) + block(place + 2 + step, False).astype(jnp.float32)
        one, two = one.astype(jnp.bfloat16), two.astype(jnp.bfloat16)
    return jnp.concatenate([one, two], axis=0)


def gather_blocks(own, order, place):
    size, rows = len(order), own.shape[0]
    half = rows // 2
    table = jnp.array(order, jnp.int32)
    ahead = [(order[i], order[(i + 1) % size]) for i in range(size)]
    back = [(b, a) for a, b in ahead]
    whole = jnp.zeros((size * rows, own.shape[1]), own.dtype)
    whole = lax.dynamic_update_slice_in_dim(whole, own, table[place] * rows, 0)
    one, two = own[:half], own[half:]
    for step in range(1, size):
        one = lax.ppermute(one, "row", ahead)
        two = lax.ppermute(two, "row", back)
        first = table[(place - step + size) % size] * rows
        second = table[(place + step) % size] * rows + half
        whole = lax.dynamic_update_slice_in_dim(whole, one, first, 0)
        whole = lax.dynamic_update_slice_in_dim(whole, two, second, 0)
    return whole


def inverse_root_of(gram_scaled):
    identity = jnp.eye(gram_scaled.shape[0], dtype=jnp.float32)
    iterate_y = gram_scaled.astype(jnp.bfloat16)
    turn = ((3.0 * identity - iterate_y.astype(jnp.float32)) * 0.5).astype(jnp.bfloat16)
    iterate_y = dot16(iterate_y, turn)
    iterate_z = turn
    for iteration in range(1, NS_STEPS):
        turn = ((3.0 * identity - dot32(iterate_z, iterate_y)) * 0.5).astype(jnp.bfloat16)
        if iteration + 1 < NS_STEPS:
            iterate_y = dot16(turn, iterate_y)
        iterate_z = dot16(turn, iterate_z)
    return iterate_z


def body(deltas, sketch):
    local_tasks, local_rows, model_width = deltas.shape
    row_devices = lax.axis_size("row")
    groups = lax.axis_size("task")
    task = lax.axis_index("task")
    rank_width = sketch.shape[1]
    width = local_tasks * rank_width
    order = ring_order(row_devices)
    inverse = [order.index(i) for i in range(row_devices)]
    place = jnp.array(inverse, jnp.int32)[lax.axis_index("row")]
    terms = jnp.einsum("tmk,mr->ktr", deltas, sketch, preferred_element_type=jnp.float32)
    terms = terms.reshape(row_devices, model_width // row_devices, width).astype(jnp.bfloat16)
    pooled = deltas[0].astype(jnp.float32)
    for slot in range(1, local_tasks):
        pooled = pooled + deltas[slot].astype(jnp.float32)
    pooled = pooled.astype(jnp.bfloat16)

    basis_local = reduce_blocks(terms, order, place)
    parts = [basis_local]
    bit = 2
    while bit < groups:
        other = [swap(part, bit, groups) for part in parts]
        upper = (task // bit) % 2 == 1
        parts = [jnp.where(upper, b, a) for a, b in zip(parts, other)] + [
            jnp.where(upper, a, b) for a, b in zip(parts, other)
        ]
        bit *= 2
    near = gather_blocks(jnp.concatenate(parts, axis=1), order, place)
    far = swap(near, 1, groups)

    near_part = dot16(pooled, near)
    sent = swap(near_part, 1, groups)
    far_part = dot32(pooled, far)
    chip_sum = (far_part + sent.astype(jnp.float32)).astype(jnp.bfloat16)

    chunk = local_rows // ROW_CHUNKS
    coeffs = []
    for at in range(ROW_CHUNKS):
        far_sum = chip_sum[at * chunk : (at + 1) * chunk]
        bit = 2
        while bit < groups:
            other = swap(far_sum, bit, groups).astype(jnp.float32)
            far_sum = (far_sum.astype(jnp.float32) + other).astype(jnp.bfloat16)
            bit *= 2
        coeffs.append((swap(far_sum, 1, groups), far_sum))

    basis = jnp.concatenate([near, far], axis=1)
    gram = lax.dot_general(basis, basis, (((0,), (0,)), ((), ())), preferred_element_type=jnp.float32)
    frob = jnp.sqrt(jnp.sum(gram * gram))
    root = inverse_root_of(gram / frob)
    columns = model_width // groups
    column_basis = lax.dynamic_slice_in_dim(basis, task * columns, columns, 0)
    left = lax.dot_general(
        root, column_basis, (((1,), (1,)), ((), ())), preferred_element_type=jnp.float32
    ).astype(jnp.bfloat16)
    left = (dot32(root, left) / (frob * (local_tasks * groups))).astype(jnp.bfloat16)
    coeff = jnp.concatenate([jnp.concatenate(pair, axis=1) for pair in coeffs], axis=0)
    return dot16(coeff, left)


def solution(mesh):
    return jax.shard_map(
        body,
        mesh=mesh,
        in_specs=(P("task", "row", None), P("row", None)),
        out_specs=P("row", "task"),
        check_vma=False,
    )
```

time: 989 us -> 448 us (0.45)
  waiting for transfers between devices: 768 us -> 114 us
  local copies, waits for them, and re-layouts: 5.6 us -> 50 us
  starting transfers between devices: 0.94 us -> 38.5 us
  between operations: 14.1 us -> 43.2 us
  blocking collectives: 26 us -> 0 us
  matrix products: 172 us -> 184 us
    all_gather x11 -> x0, waiting for transfers between devices: 510 us -> none  [the longest x1 148 us: body(): basis_whole = lax.all_gather(basis_block, 'row', axis=0, tiled=True)]
    psum x1 -> x0, waiting for transfers between devices: 121 us -> none  [body(): lax.psum(coeff_part.astype(jnp.bfloat16), 'task').astype(jnp.float32)]
    ppermute x0 -> x39, waiting for transfers between devices: none -> 114 us  [the longest x11 64.6 us: swap(): return lax.ppermute(value, 'task', [(i, i ^ bit) for i in range(size)])]
    unnamed x15 -> x0, waiting for transfers between devices: 74 us -> none
    reduce_scatter x1 -> x0, waiting for transfers between devices: 62.9 us -> none  [body(): lax.psum_scatter(jnp.einsum('kc,kp->cp', basis_block, basis_local, prefer...]
    ppermute x0 -> x39, starting transfers between devices: none -> 38.5 us  [the longest x7 15.3 us: reduce_blocks(): one = lax.ppermute(one, 'row', ahead)]
    psum x1 -> x0, blocking collectives: 20.1 us -> none  [body(): frob = jnp.sqrt(lax.psum(jnp.sum(gram_own * gram_own), 'row'))]
    unnamed x20 -> x45, local copies, waits for them, and re-layouts: 5.6 us -> 20.7 us
  transfers between devices with their start and end apart: 14 -> 39, of which waited for: 13 -> 26; matrix products, arithmetic and copies ran while one was open for 11% -> 29% of each run, Pallas kernels for 0% -> 0%
where the time goes in v1:
time: 448 us; the launch traced here: 439 us
  matrix products  184 us (41%)
  waiting for transfers between devices  114 us (25%)
  local copies, waits for them, and re-layouts  50 us (11%)
  between operations  43.2 us (10%)
  starting transfers between devices  38.5 us (9%)
  other arithmetic  9.34 us (2%)
    dot_general x14, matrix products, dot32(): return jnp.dot(a, b, preferred_element_type=jnp.float32)  130 us
    ppermute x11, waiting for transfers between devices, swap(): return lax.ppermute(value, 'task', [(i, i ^ bit) for i in range(size)])  64.6 us
    dot_general x1, matrix products, body(): jnp.einsum('tmk,mr->ktr', deltas, sketch, preferred_element_type=jnp.floa...  25.7 us
    ppermute x7, waiting for transfers between devices, gather_blocks(): one = lax.ppermute(one, 'row', ahead)  24.9 us
    dot_general x1, matrix products, body(): lax.dot_general(basis, basis, (((0,), (0,)), ((), ())), preferred_element...  20.8 us
    unnamed x45, local copies, waits for them, and re-layouts  20.7 us
    ppermute x7, waiting for transfers between devices, reduce_blocks(): one = lax.ppermute(one, 'row', ahead)  17.6 us
    ppermute x7, starting transfers between devices, reduce_blocks(): one = lax.ppermute(one, 'row', ahead)  15.3 us
  transfers between devices with their start and end apart: 39, of which 26 were waited for; matrix products, arithmetic and copies ran while one was open for 29% of the time, Pallas kernels for 0%

profile of v1, /device:TPU:0, one launch (start us, length us, event | category | flops | bytes accessed | tf_op | source)
XLA Modules:
  0.0 438.8 jit_solution(18209113044698928111)
XLA Ops:
  31.4 25.7 %convolution_convert_fusion.1 = bf16[128,2,5120]{2,0,1:T(8,128)(2,1)} fusion(bf16[2,3200,5120]{2,1,0:T(8,128)(2,1)} %param.5, bf16[3200,128]{1,0:T(8,128)(2,1)S(1)} %copy-done), kind=kOutput, calls=%fused_computation.28 | convolution fusion | flops 8389918720 | bytes 68976640 | tf_op jit(solution)/shard_map/tmk,mr->ktr/dot_general | solution.py:91
  68.1 10.6 %constant_dynamic-slice_fusion = (bf16[1,320,256]{1,0,2:T(2,128)(2,1)}, bf16[1,320,256]{1,0,2:T(2,128)(2,1)}, bf16[1,320,256]{1,0,2:T(2,128)(2,1)}, bf16[1,320,2...) fusion(bf16[8,640,256]{1,0,2:T(8,128)(2,1)S(1)} %bitcast.106, ...), kind=kLoop, calls=%fused_computation.104 | loop fusion | bytes 5242940 | tf_op jit(solution)/shard_map/slice | solution.py:35
  80.7 3.0 collective-permute-start
  104.8 2.5 collective-permute-done.1
  116.8 3.1 collective-permute-done.3
  120.0 2.5 collective-permute-start.4
  123.3 4.0 collective-permute-done.4
  130.2 3.1 collective-permute-done.5
  136.3 2.5 collective-permute-done.6
  142.8 5.6 %collective-permute-done.14 = bf16[640,256]{1,0:T(8,128)(2,1)S(1)} collective-permute-done((bf16[640,256]{1,0:T(8,128)(2,1)S(1)}, bf16[640,256]{1,0:T(8,128)(2,1)S(1)}, u32[]{:S(2)}, u32[]{:S(2)}) %collective-permute-start.14) | collective-permute-done | bytes 327712 | tf_op jit(solution)/shard_map/ppermute | solution.py:19
  150.6 6.3 %collective-permute-done.15 = bf16[320,512]{1,0:T(8,128)(2,1)S(1)} collective-permute-done((bf16[320,512]{1,0:T(8,128)(2,1)S(1)}, bf16[320,512]{1,0:T(8,128)(2,1)S(1)}, u32[]{:S(2)}, u32[]{:S(2)}) %collective-permute-start.15) | collective-permute-done | bytes 327712 | tf_op jit(solution)/shard_map/ppermute | solution.py:58
  158.9 5.4 %collective-permute-done.17 = bf16[320,512]{1,0:T(8,128)(2,1)S(1)} collective-permute-done((bf16[320,512]{1,0:T(8,128)(2,1)S(1)}, bf16[320,512]{1,0:T(8,128)(2,1)S(1)}, u32[]{:S(2)}, u32[]{:S(2)}) %collective-permute-start.17) | collective-permute-done | bytes 327712 | tf_op jit(solution)/shard_map/ppermute | solution.py:58
  171.3 2.7 broadcast_in_dim.3
  179.2 4.5 %collective-permute-done.21 = bf16[320,512]{1,0:T(8,128)(2,1)S(1)} collective-permute-done((bf16[320,512]{1,0:T(8,128)(2,1)S(1)}, bf16[320,512]{1,0:T(8,128)(2,1)S(1)}, u32[]{:S(2)}, u32[]{:S(2)}) %collective-permute-start.21) | collective-permute-done | bytes 327712 | tf_op jit(solution)/shard_map/ppermute | solution.py:58
  188.0 3.5 collective-permute-done.23
  196.0 2.6 collective-permute-done.25
  203.0 2.6 collective-permute-done.27
  208.9 28.5 %convolution_convert_fusion.2 = bf16[3200,512]{1,0:T(8,128)(2,1)} fusion(bf16[5120,512]{1,0:T(8,128)(2,1)} %constant_dynamic-update-slice_fusion, bf16[2,3200,5120]{2,1,0:T(8,128)(2,1)} %param.5), kind=kOutput, calls=%fused_computation.30 | convolution fusion | flops 16844390400 | bytes 74055680 | tf_op jit(solution)/shard_map/dot_general | solution.py:11
  238.0 20.8 %multiply_reduce_fusion = (f32[]{:T(128)}, f32[1024,1024]{1,0:T(8,128)}) fusion(bf16[5120,512]{1,0:T(8,128)(2,1)} %collective-permute-done.29, bf16[5120,512]{1,0:T(8,128)(2,1)} %constant_dynamic-update-slice_fusion), kind=kOutput, calls=%fused_computation.43 | convolution fusion | flops 10760486912 | bytes 14680068 | tf_op jit(solution)/shard_map/dot_general | solution.py:128
  259.4 2.8 divide_convert_fusion.1
  262.2 2.6 convolution_convert_fusion.9
  276.6 3.7 convolution_convert_fusion.6
  280.3 33.7 %fusion.17 = bf16[3200,512]{1,0:T(8,128)(2,1)} fusion(bf16[3200,512]{1,0:T(8,128)(2,1)} %collective-permute-done.30, bf16[5120,512]{1,0:T(8,128)(2,1)} %collective-permute-done.29, bf16[2,3200,5120]{2,1,0:T(8,128)(2,1)} %param.5), kind=kOutput, calls=%fused_computation.29 | convolution fusion | flops 16847667200 | bytes 77332480 | tf_op jit(solution)/shard_map/dot_general | solution.py:11
  322.7 3.7 fusion.85
  326.4 3.7 convolution_convert_fusion.4
  330.1 7.3 %collective-permute-done.31 = bf16[800,512]{1,0:T(8,128)(2,1)S(1)} collective-permute-done((bf16[800,512]{1,0:T(8,128)(2,1)S(1)}, bf16[800,512]{1,0:T(8,128)(2,1)S(1)}, u32[]{:S(2)}, u32[]{:S(2)}) %collective-permute-start.31) | collective-permute-done | bytes 819232 | tf_op jit(solution)/shard_map/ppermute | solution.py:19
  337.4 17.6 %collective-permute-done.33 = bf16[800,512]{1,0:T(8,128)(2,1)S(1)} collective-permute-done((bf16[800,512]{1,0:T(8,128)(2,1)S(1)}, bf16[800,512]{1,0:T(8,128)(2,1)S(1)}, u32[]{:S(2)}, u32[]{:S(2)}) %collective-permute-start.33) | collective-permute-done | bytes 819232 | tf_op jit(solution)/shard_map/ppermute | solution.py:19
  355.0 17.6 %collective-permute-done.35 = bf16[800,512]{1,0:T(8,128)(2,1)S(1)} collective-permute-done((bf16[800,512]{1,0:T(8,128)(2,1)S(1)}, bf16[800,512]{1,0:T(8,128)(2,1)S(1)}, u32[]{:S(2)}, u32[]{:S(2)}) %collective-permute-start.35) | collective-permute-done | bytes 819232 | tf_op jit(solution)/shard_map/ppermute | solution.py:19
  372.5 16.6 %collective-permute-done.37 = bf16[800,512]{1,0:T(8,128)(2,1)S(1)} collective-permute-done((bf16[800,512]{1,0:T(8,128)(2,1)S(1)}, bf16[800,512]{1,0:T(8,128)(2,1)S(1)}, u32[]{:S(2)}, u32[]{:S(2)}) %collective-permute-start.37) | collective-permute-done | bytes 819232 | tf_op jit(solution)/shard_map/ppermute | solution.py:19
  391.4 8.8 %fusion.39 = bf16[1024,1024]{1,0:T(8,128)(2,1)} fusion(bf16[1024,1024]{1,0:T(8,128)(2,1)} %convolution_convert_fusion.4, bf16[1024,1024]{1,0:T(8,128)(2,1)} %fusion.85), kind=kOutput, calls=%fused_computation.53 | convolution fusion | flops 4301258752 | bytes 6291456 | tf_op jit(solution)/shard_map/dot_general | solution.py:11
  400.1 6.8 %convolution_convert_fusion.3 = bf16[1024,1280]{1,0:T(8,128)(2,1)} fusion(bf16[1024,1024]{1,0:T(8,128)(2,1)} %fusion.39, s32[]{:T(128)S(6)} %select_n.332, bf16[5120,512]{1,0:T(8,128)(2,1)} %constant_dynamic-update-slice_fusion, bf16[5120,512]{1,0:T(8,128)(2,1)} %collective-permute-done.29), kind=kOutput, calls=%fused_computation.45 | convolution fusion | flops 2690908160 | bytes 15204356 | tf_op jit(solution)/shard_map/dot_general | solution.py:133
  406.9 31.7 %convolution_convert_fusion = bf16[3200,1280]{1,0:T(8,128)(2,1)} fusion(bf16[800,512]{1,0:T(8,128)(2,1)} %copy-done.9, bf16[800,512]{1,0:T(8,128)(2,1)} %collective-permute-done.38, bf16[800,512]{1,0:T(8,128)(2,1)S(1)} %get-tuple-element.7, bf16[800,512]{1,0:T(8,128)(2,1)} %collective-permute-done.36, bf16[800,512]{1,0:T(8,128)(2,1)S(1)} %get-tuple-element.6, ...), kind=kOutput, calls=%fused_computation.2 | convolution fusion | flops 11132108800 | bytes 19464196 | tf_op jit(solution)/shard_map/dot_general | solution.py:11
  (147 shorter events, 99.6 us)
Async XLA Ops:
  80.7 19.9 %collective-permute-start = (bf16[320,256]{1,0:T(8,128)(2,1)}, bf16[320,256]{1,0:T(8,128)(2,1)}, u32[]{:S(2)}, u32[]{:S(2)}) collective-permute-start(bf16[320,256]{1,0:T(8,128)(2,1)} %bitcast.5), channel_id=1, source_target_pairs={{0,2},{2,4},{4,6},{6,7},{7,5},{5,3},{3,1},{1,0},{8,10},{10,12},{12... | collective-permute-start | bytes 491528 | tf_op jit(solution)/shard_map/ppermute | solution.py:40
  85.5 18.1 %collective-permute-start.7 = (bf16[320,256]{1,0:T(8,128)(2,1)}, bf16[320,256]{1,0:T(8,128)(2,1)}, u32[]{:S(2)}, u32[]{:S(2)}) collective-permute-start(bf16[320,256]{1,0:T(8,128)(2,1)} %bitcast.21), channel_id=1, source_target_pairs={{2,0},{4,2},{6,4},{7,6},{5,7},{3,5},{1,3},{0,1},{10,8},{12,10},{14... | collective-permute-start | bytes 491528 | tf_op jit(solution)/shard_map/ppermute | solution.py:41
  113.7 6.2 %collective-permute-start.3 = (bf16[320,256]{1,0:T(8,128)(2,1)S(1)}, bf16[320,256]{1,0:T(8,128)(2,1)S(1)}, u32[]{:S(2)}, u32[]{:S(2)}) collective-permute-start(bf16[320,256]{1,0:T(8,128)(2,1)S(1)} %fusion.64), channel_id=1, source_target_pairs={{0,2},{2,4},{4,6},{6,7},{7,5},{5,3},{3,1},{1,0},{8,10},{10,12},{12... | collective-permute-start | bytes 491528 | tf_op jit(solution)/shard_map/ppermute | solution.py:40
  116.7 6.5 %collective-permute-start.10 = (bf16[320,256]{1,0:T(8,128)(2,1)S(1)}, bf16[320,256]{1,0:T(8,128)(2,1)S(1)}, u32[]{:S(2)}, u32[]{:S(2)}) collective-permute-start(bf16[320,256]{1,0:T(8,128)(2,1)S(1)} %fusion.57), channel_id=1, source_target_pairs={{2,0},{4,2},{6,4},{7,6},{5,7},{3,5},{1,3},{0,1},{10,8},{12,10},{14... | collective-permute-start | bytes 491528 | tf_op jit(solution)/shard_map/ppermute | solution.py:41
  120.0 7.4 %collective-permute-start.4 = (bf16[320,256]{1,0:T(8,128)(2,1)S(1)}, bf16[320,256]{1,0:T(8,128)(2,1)S(1)}, u32[]{:S(2)}, u32[]{:S(2)}) collective-permute-start(bf16[320,256]{1,0:T(8,128)(2,1)S(1)} %fusion.63), channel_id=1, source_target_pairs={{0,2},{2,4},{4,6},{6,7},{7,5},{5,3},{3,1},{1,0},{8,10},{10,12},{12... | collective-permute-start | bytes 491528 | tf_op jit(solution)/shard_map/ppermute | solution.py:40
  123.3 6.6 %collective-permute-start.11 = (bf16[320,256]{1,0:T(8,128)(2,1)S(1)}, bf16[320,256]{1,0:T(8,128)(2,1)S(1)}, u32[]{:S(2)}, u32[]{:S(2)}) collective-permute-start(bf16[320,256]{1,0:T(8,128)(2,1)S(1)} %fusion.56), channel_id=1, source_target_pairs={{2,0},{4,2},{6,4},{7,6},{5,7},{3,5},{1,3},{0,1},{10,8},{12,10},{14... | collective-permute-start | bytes 491528 | tf_op jit(solution)/shard_map/ppermute | solution.py:41
  127.4 6.0 %collective-permute-start.5 = (bf16[320,256]{1,0:T(8,128)(2,1)S(1)}, bf16[320,256]{1,0:T(8,128)(2,1)S(1)}, u32[]{:S(2)}, u32[]{:S(2)}) collective-permute-start(bf16[320,256]{1,0:T(8,128)(2,1)S(1)} %fusion.62), channel_id=1, source_target_pairs={{0,2},{2,4},{4,6},{6,7},{7,5},{5,3},{3,1},{1,0},{8,10},{10,12},{12... | collective-permute-start | bytes 491528 | tf_op jit(solution)/shard_map/ppermute | solution.py:40
  141.2 7.1 %collective-permute-start.14 = (bf16[640,256]{1,0:T(8,128)(2,1)S(1)}, bf16[640,256]{1,0:T(8,128)(2,1)S(1)}, u32[]{:S(2)}, u32[]{:S(2)}) collective-permute-start(bf16[640,256]{1,0:T(8,128)(2,1)S(1)} %pad_maximum_fusion.3), channel_id=1, source_target_pairs={{0,16},{8,24},{16,0},{24,8},{1,17},{9,25},{17,1},{25,9},{2,18},{10... | collective-permute-start | bytes 983048 | tf_op jit(solution)/shard_map/ppermute | solution.py:19
  148.5 8.4 %collective-permute-start.15 = (bf16[320,512]{1,0:T(8,128)(2,1)S(1)}, bf16[320,512]{1,0:T(8,128)(2,1)S(1)}, u32[]{:S(2)}, u32[]{:S(2)}) collective-permute-start(bf16[320,512]{1,0:T(8,128)(2,1)S(1)} %get-tuple-element.30), channel_id=1, source_target_pairs={{0,2},{2,4},{4,6},{6,7},{7,5},{5,3},{3,1},{1,0},{8,10},{10,12},{12... | collective-permute-start | bytes 983048 | tf_op jit(solution)/shard_map/ppermute | solution.py:58
  150.1 8.3 %collective-permute-start.16 = (bf16[320,512]{1,0:T(8,128)(2,1)S(1)}, bf16[320,512]{1,0:T(8,128)(2,1)S(1)}, u32[]{:S(2)}, u32[]{:S(2)}) collective-permute-start(bf16[320,512]{1,0:T(8,128)(2,1)S(1)} %get-tuple-element.29), channel_id=1, source_target_pairs={{2,0},{4,2},{6,4},{7,6},{5,7},{3,5},{1,3},{0,1},{10,8},{12,10},{14... | collective-permute-start | bytes 983048 | tf_op jit(solution)/shard_map/ppermute | solution.py:59
  156.9 7.4 %collective-permute-start.17 = (bf16[320,512]{1,0:T(8,128)(2,1)S(1)}, bf16[320,512]{1,0:T(8,128)(2,1)S(1)}, u32[]{:S(2)}, u32[]{:S(2)}) collective-permute-start(bf16[320,512]{1,0:T(8,128)(2,1)S(1)} %collective-permute-done.15), channel_id=1, source_target_pairs={{0,2},{2,4},{4,6},{6,7},{7,5},{5,3},{3,1},{1,0},{8,10},{10,12},{12... | collective-permute-start | bytes 983048 | tf_op jit(solution)/shard_map/ppermute | solution.py:58
  158.5 7.4 %collective-permute-start.18 = (bf16[320,512]{1,0:T(8,128)(2,1)S(1)}, bf16[320,512]{1,0:T(8,128)(2,1)S(1)}, u32[]{:S(2)}, u32[]{:S(2)}) collective-permute-start(bf16[320,512]{1,0:T(8,128)(2,1)S(1)} %collective-permute-done.16), channel_id=1, source_target_pairs={{2,0},{4,2},{6,4},{7,6},{5,7},{3,5},{1,3},{0,1},{10,8},{12,10},{14... | collective-permute-start | bytes 983048 | tf_op jit(solution)/shard_map/ppermute | solution.py:59
  164.3 10.6 %collective-permute-start.19 = (bf16[320,512]{1,0:T(8,128)(2,1)S(1)}, bf16[320,512]{1,0:T(8,128)(2,1)S(1)}, u32[]{:S(2)}, u32[]{:S(2)}) collective-permute-start(bf16[320,512]{1,0:T(8,128)(2,1)S(1)} %collective-permute-done.17), channel_id=1, source_target_pairs={{0,2},{2,4},{4,6},{6,7},{7,5},{5,3},{3,1},{1,0},{8,10},{10,12},{12... | collective-permute-start | bytes 983048 | tf_op jit(solution)/shard_map/ppermute | solution.py:58
  165.9 11.4 %collective-permute-start.20 = (bf16[320,512]{1,0:T(8,128)(2,1)S(1)}, bf16[320,512]{1,0:T(8,128)(2,1)S(1)}, u32[]{:S(2)}, u32[]{:S(2)}) collective-permute-start(bf16[320,512]{1,0:T(8,128)(2,1)S(1)} %collective-permute-done.18), channel_id=1, source_target_pairs={{2,0},{4,2},{6,4},{7,6},{5,7},{3,5},{1,3},{0,1},{10,8},{12,10},{14... | collective-permute-start | bytes 983048 | tf_op jit(solution)/shard_map/ppermute | solution.py:59
  174.9 8.7 %collective-permute-start.21 = (bf16[320,512]{1,0:T(8,128)(2,1)S(1)}, bf16[320,512]{1,0:T(8,128)(2,1)S(1)}, u32[]{:S(2)}, u32[]{:S(2)}) collective-permute-start(bf16[320,512]{1,0:T(8,128)(2,1)S(1)} %collective-permute-done.19), channel_id=1, source_target_pairs={{0,2},{2,4},{4,6},{6,7},{7,5},{5,3},{3,1},{1,0},{8,10},{10,12},{12... | collective-permute-start | bytes 983048 | tf_op jit(solution)/shard_map/ppermute | solution.py:58
  177.2 8.9 %collective-permute-start.22 = (bf16[320,512]{1,0:T(8,128)(2,1)S(1)}, bf16[320,512]{1,0:T(8,128)(2,1)S(1)}, u32[]{:S(2)}, u32[]{:S(2)}) collective-permute-start(bf16[320,512]{1,0:T(8,128)(2,1)S(1)} %collective-permute-done.20), channel_id=1, source_target_pairs={{2,0},{4,2},{6,4},{7,6},{5,7},{3,5},{1,3},{0,1},{10,8},{12,10},{14... | collective-permute-start | bytes 983048 | tf_op jit(solution)/shard_map/ppermute | solution.py:59
  183.7 7.9 %collective-permute-start.23 = (bf16[320,512]{1,0:T(8,128)(2,1)S(1)}, bf16[320,512]{1,0:T(8,128)(2,1)S(1)}, u32[]{:S(2)}, u32[]{:S(2)}) collective-permute-start(bf16[320,512]{1,0:T(8,128)(2,1)S(1)} %collective-permute-done.21), channel_id=1, source_target_pairs={{0,2},{2,4},{4,6},{6,7},{7,5},{5,3},{3,1},{1,0},{8,10},{10,12},{12... | collective-permute-start | bytes 983048 | tf_op jit(solution)/shard_map/ppermute | solution.py:58
  186.1 7.9 %collective-permute-start.24 = (bf16[320,512]{1,0:T(8,128)(2,1)S(1)}, bf16[320,512]{1,0:T(8,128)(2,1)S(1)}, u32[]{:S(2)}, u32[]{:S(2)}) collective-permute-start(bf16[320,512]{1,0:T(8,128)(2,1)S(1)} %collective-permute-done.22), channel_id=1, source_target_pairs={{2,0},{4,2},{6,4},{7,6},{5,7},{3,5},{1,3},{0,1},{10,8},{12,10},{14... | collective-permute-start | bytes 983048 | tf_op jit(solution)/shard_map/ppermute | solution.py:59
  191.5 7.1 %collective-permute-start.25 = (bf16[320,512]{1,0:T(8,128)(2,1)S(1)}, bf16[320,512]{1,0:T(8,128)(2,1)S(1)}, u32[]{:S(2)}, u32[]{:S(2)}) collective-permute-start(bf16[320,512]{1,0:T(8,128)(2,1)S(1)} %collective-permute-done.23), channel_id=1, source_target_pairs={{0,2},{2,4},{4,6},{6,7},{7,5},{5,3},{3,1},{1,0},{8,10},{10,12},{12... | collective-permute-start | bytes 983048 | tf_op jit(solution)/shard_map/ppermute | solution.py:58
  194.0 7.1 %collective-permute-start.26 = (bf16[320,512]{1,0:T(8,128)(2,1)S(1)}, bf16[320,512]{1,0:T(8,128)(2,1)S(1)}, u32[]{:S(2)}, u32[]{:S(2)}) collective-permute-start(bf16[320,512]{1,0:T(8,128)(2,1)S(1)} %collective-permute-done.24), channel_id=1, source_target_pairs={{2,0},{4,2},{6,4},{7,6},{5,7},{3,5},{1,3},{0,1},{10,8},{12,10},{14... | collective-permute-start | bytes 983048 | tf_op jit(solution)/shard_map/ppermute | solution.py:59
  198.6 7.1 %collective-permute-start.27 = (bf16[320,512]{1,0:T(8,128)(2,1)S(1)}, bf16[320,512]{1,0:T(8,128)(2,1)S(1)}, u32[]{:S(2)}, u32[]{:S(2)}) collective-permute-start(bf16[320,512]{1,0:T(8,128)(2,1)S(1)} %collective-permute-done.25), channel_id=1, source_target_pairs={{0,2},{2,4},{4,6},{6,7},{7,5},{5,3},{3,1},{1,0},{8,10},{10,12},{12... | collective-permute-start | bytes 983048 | tf_op jit(solution)/shard_map/ppermute | solution.py:58
  201.1 7.1 %collective-permute-start.28 = (bf16[320,512]{1,0:T(8,128)(2,1)S(1)}, bf16[320,512]{1,0:T(8,128)(2,1)S(1)}, u32[]{:S(2)}, u32[]{:S(2)}) collective-permute-start(bf16[320,512]{1,0:T(8,128)(2,1)S(1)} %collective-permute-done.26), channel_id=1, source_target_pairs={{2,0},{4,2},{6,4},{7,6},{5,7},{3,5},{1,3},{0,1},{10,8},{12,10},{14... | collective-permute-start | bytes 983048 | tf_op jit(solution)/shard_map/ppermute | solution.py:59
  208.9 29.1 %collective-permute-start.29 = (bf16[5120,512]{1,0:T(8,128)(2,1)}, bf16[5120,512]{1,0:T(8,128)(2,1)}, u32[]{:S(2)}, u32[]{:S(2)}) collective-permute-start(bf16[5120,512]{1,0:T(8,128)(2,1)} %constant_dynamic-update-slice_fusion), channel_id=1, source_target_pairs={{0,8},{8,0},{16,24},{24,16},{1,9},{9,1},{17,25},{25,17},{2,10},{10... | collective-permute-start | bytes 15728648 | tf_op jit(solution)/shard_map/ppermute | solution.py:19
  237.4 42.8 %collective-permute-start.30 = (bf16[3200,512]{1,0:T(8,128)(2,1)}, bf16[3200,512]{1,0:T(8,128)(2,1)}, u32[]{:S(2)}, u32[]{:S(2)}) collective-permute-start(bf16[3200,512]{1,0:T(8,128)(2,1)} %convolution_convert_fusion.2), channel_id=1, source_target_pairs={{0,8},{8,0},{16,24},{24,16},{1,9},{9,1},{17,25},{25,17},{2,10},{10... | collective-permute-start | bytes 9830408 | tf_op jit(solution)/shard_map/ppermute | solution.py:19
  316.2 21.2 %collective-permute-start.31 = (bf16[800,512]{1,0:T(8,128)(2,1)S(1)}, bf16[800,512]{1,0:T(8,128)(2,1)S(1)}, u32[]{:S(2)}, u32[]{:S(2)}) collective-permute-start(bf16[800,512]{1,0:T(8,128)(2,1)S(1)} %get-tuple-element.9), channel_id=1, source_target_pairs={{0,16},{8,24},{16,0},{24,8},{1,17},{9,25},{17,1},{25,9},{2,18},{10... | collective-permute-start | bytes 2457608 | tf_op jit(solution)/shard_map/ppermute | solution.py:19
  317.8 37.1 %collective-permute-start.33 = (bf16[800,512]{1,0:T(8,128)(2,1)S(1)}, bf16[800,512]{1,0:T(8,128)(2,1)S(1)}, u32[]{:S(2)}, u32[]{:S(2)}) collective-permute-start(bf16[800,512]{1,0:T(8,128)(2,1)S(1)} %get-tuple-element.12), channel_id=1, source_target_pairs={{0,16},{8,24},{16,0},{24,8},{1,17},{9,25},{17,1},{25,9},{2,18},{10... | collective-permute-start | bytes 2457608 | tf_op jit(solution)/shard_map/ppermute | solution.py:19
  318.3 54.2 %collective-permute-start.35 = (bf16[800,512]{1,0:T(8,128)(2,1)S(1)}, bf16[800,512]{1,0:T(8,128)(2,1)S(1)}, u32[]{:S(2)}, u32[]{:S(2)}) collective-permute-start(bf16[800,512]{1,0:T(8,128)(2,1)S(1)} %get-tuple-element.11), channel_id=1, source_target_pairs={{0,16},{8,24},{16,0},{24,8},{1,17},{9,25},{17,1},{25,9},{2,18},{10... | collective-permute-start | bytes 2457608 | tf_op jit(solution)/shard_map/ppermute | solution.py:19
  319.8 69.3 %collective-permute-start.37 = (bf16[800,512]{1,0:T(8,128)(2,1)S(1)}, bf16[800,512]{1,0:T(8,128)(2,1)S(1)}, u32[]{:S(2)}, u32[]{:S(2)}) collective-permute-start(bf16[800,512]{1,0:T(8,128)(2,1)S(1)} %get-tuple-element.10), channel_id=1, source_target_pairs={{0,16},{8,24},{16,0},{24,8},{1,17},{9,25},{17,1},{25,9},{2,18},{10... | collective-permute-start | bytes 2457608 | tf_op jit(solution)/shard_map/ppermute | solution.py:19
  390.3 16.6 %collective-permute-start.32 = (bf16[800,512]{1,0:T(8,128)(2,1)S(1)}, bf16[800,512]{1,0:T(8,128)(2,1)}, u32[]{:S(2)}, u32[]{:S(2)}) collective-permute-start(bf16[800,512]{1,0:T(8,128)(2,1)S(1)} %get-tuple-element.5), channel_id=1, source_target_pairs={{0,8},{8,0},{16,24},{24,16},{1,9},{9,1},{17,25},{25,17},{2,10},{10... | collective-permute-start | bytes 2457608 | tf_op jit(solution)/shard_map/ppermute | solution.py:19
  390.3 16.6 %collective-permute-start.34 = (bf16[800,512]{1,0:T(8,128)(2,1)S(1)}, bf16[800,512]{1,0:T(8,128)(2,1)}, u32[]{:S(2)}, u32[]{:S(2)}) collective-permute-start(bf16[800,512]{1,0:T(8,128)(2,1)S(1)} %get-tuple-element.6), channel_id=1, source_target_pairs={{0,8},{8,0},{16,24},{24,16},{1,9},{9,1},{17,25},{25,17},{2,10},{10... | collective-permute-start | bytes 2457608 | tf_op jit(solution)/shard_map/ppermute | solution.py:19
  390.8 16.1 %collective-permute-start.36 = (bf16[800,512]{1,0:T(8,128)(2,1)S(1)}, bf16[800,512]{1,0:T(8,128)(2,1)}, u32[]{:S(2)}, u32[]{:S(2)}) collective-permute-start(bf16[800,512]{1,0:T(8,128)(2,1)S(1)} %get-tuple-element.7), channel_id=1, source_target_pairs={{0,8},{8,0},{16,24},{24,16},{1,9},{9,1},{17,25},{25,17},{2,10},{10... | collective-permute-start | bytes 2457608 | tf_op jit(solution)/shard_map/ppermute | solution.py:19
  390.9 16.0 %collective-permute-start.38 = (bf16[800,512]{1,0:T(8,128)(2,1)S(1)}, bf16[800,512]{1,0:T(8,128)(2,1)}, u32[]{:S(2)}, u32[]{:S(2)}) collective-permute-start(bf16[800,512]{1,0:T(8,128)(2,1)S(1)} %get-tuple-element.8), channel_id=1, source_target_pairs={{0,8},{8,0},{16,24},{24,16},{1,9},{9,1},{17,25},{25,17},{2,10},{10... | collective-permute-start | bytes 2457608 | tf_op jit(solution)/shard_map/ppermute | solution.py:19
  (21 other events, 363.8 us)
